TPU v7x, 32 devices: a whole 2x2x4 slice. The times are simulated.
32 devices in a mesh: pair: 16 (over z, y, x), virt: 2 (over core).
Axes of the slice: x: 2, y: 2, z: 4, core: 2. Of those that a mesh axis runs over, the one named last changes fastest.
Arguments:
- t2_amplitudes: float32 [64, 2048], P('pair', 'virt'), may hold values from -6 to 6
- integral_tiles: float32 [16, 2, 32, 128, 128], P('pair', 'virt'), may hold values from -0.125 to 0.125
- out_tiles: int32 [16, 2, 32], P('pair', 'virt'), may hold values from 0 to 15, as said below
- in_tiles: int32 [16, 2, 32], P('pair', 'virt'), may hold values from 0 to 15
- tile_counts: int32 [16, 2], P('pair', 'virt'), may hold values from 1 to 32, as said below
Outputs:
- ladder: float32 [64, 2048], P('pair', 'virt')
Inputs may be any that keep to these rules, and one draw needn't show every extreme that they name: `out_tiles`: slots of the devices at virt index v name output tiles v * 8 to (v + 1) * 8 - 1 only. `tile_counts`: in every draw some device has all 32 slots live.
All inputs are finite; a program needn't handle non-finite values.
Results may differ from a plain program's by a relative error of at most 0.0003.
Values sent between devices are 32-bit elements; how exact they have to be, the bound alone decides.
No kernel may reach another device: no remote copies, remote signals or barrier semaphores. Data moves between devices by JAX's collectives and lax.ppermute only.
A program may use at most 64 MiB of HBM per device.

v0:
```python
import jax
import jax.numpy as jnp
from jax import lax
from jax.experimental import pallas as pl
from jax.experimental.pallas import tpu as pltpu
from jax.sharding import PartitionSpec as P

W = 128
GROUP = 8
NEAR = 4
SMEM = pl.BlockSpec(memory_space=pltpu.SMEM)
VMEM = pl.BlockSpec(memory_space=pltpu.VMEM)


def split(value):
    high = value.astype(jnp.bfloat16)
    low = (value - high.astype(jnp.float32)).astype(jnp.bfloat16)
    return high, low


def tile_kernel(out_tiles, live, ins, outs, tiles, mine, halves, codes, own, held, index_rows, arrived, singles):
    singles_of = ((ins, index_rows.at[0]), (outs, index_rows.at[1]), (mine, own))
    others = [pltpu.make_async_copy(here, there, singles.at[at]) for at, (here, there) in enumerate(singles_of)]
    for copy in others:
        copy.start()
    count = live[0, 0]
    groups = (count + GROUP - 1) // GROUP

    def tile_copy(index):
        part = pl.ds(index * GROUP, GROUP)
        return pltpu.make_async_copy(tiles.at[part], held.at[part], arrived.at[index])

    def begin(index, carry):
        tile_copy(index).start()
        return carry

    lax.fori_loop(0, groups, begin, 0)
    for copy in others:
        copy.wait()
    slots = lax.broadcasted_iota(jnp.int32, ins.shape, 1)
    codes[0:1, :] = index_rows[0]
    codes[1:2, :] = jnp.where(slots < count, lax.rem(index_rows[1], out_tiles), out_tiles)
    codes[2:3, :] = jnp.full(ins.shape, count, jnp.int32)

    def one_group(index, carry):
        tile_copy(index).wait()
        for step in range(GROUP):
            slot = index * GROUP + step
            high, low = split(held[slot])
            halves[slot, :, :W] = high
            halves[slot, :, W:] = low
        return carry

    lax.fori_loop(0, groups, one_group, 0)


def prepare(tiles, ins, outs, live, mine, out_tiles):
    slots = tiles.shape[0]

    def kernel(*refs):
        tile_kernel(out_tiles, *refs)

    operands = [pltpu.with_memory_space_constraint(value, pltpu.HBM) for value in (ins, outs, tiles, mine)]
    return pl.pallas_call(
        kernel,
        out_shape=(
            jax.ShapeDtypeStruct((slots, W, 2 * W), jnp.bfloat16),
            jax.ShapeDtypeStruct((3, slots), jnp.int32),
            jax.ShapeDtypeStruct(mine.shape, mine.dtype),
        ),
        in_specs=[SMEM] + [pl.BlockSpec(memory_space=pltpu.HBM)] * 4,
        out_specs=(VMEM, VMEM, VMEM),
        scratch_shapes=[
            pltpu.VMEM((slots, W, W), jnp.float32),
            pltpu.VMEM((2, 1, slots), jnp.int32),
            pltpu.SemaphoreType.DMA((slots // GROUP,)),
            pltpu.SemaphoreType.DMA((3,)),
        ],
        compiler_params=pltpu.CompilerParams(vmem_limit_bytes=32 * 1024 * 1024),
        cost_estimate=pl.CostEstimate(flops=4 * slots * W * W, bytes_accessed=8 * slots * W * W, transcendentals=0),
    )(live, *operands)


def ladder_kernel(codes, blocks, halves, result, columns, flat, totals):
    owners, chunk_count = blocks.shape[:2]
    out_tiles = totals.shape[0] - 1
    rows = result.shape[1] // out_tiles
    in_local = blocks.shape[2] // rows
    totals[...] = jnp.zeros_like(totals)

    far = chunk_count // NEAR

    def spread(owner, carry):
        def one_chunk(chunk, inner):
            crossed = (chunk >= far).astype(jnp.int32) ^ (lax.rem(chunk, far) > 0).astype(jnp.int32)
            source = lax.bitwise_xor(owner, crossed)
            for tile in range(in_local):
                flat[tile, pl.ds(chunk * rows, rows), :] = blocks[source, chunk, tile * rows : (tile + 1) * rows, :]
            return inner

        lax.fori_loop(0, chunk_count, one_chunk, 0, unroll=min(chunk_count, 16))
        for tile in range(in_local):
            high, low = split(flat[tile])
            columns[owner * in_local + tile, :, :W] = high
            columns[owner * in_local + tile, :, W:] = low
        return carry

    lax.fori_loop(0, owners, spread, 0, unroll=min(owners, 2))

    def one_group(index, carry):
        first = index * GROUP
        products = []
        for step in range(GROUP):
            both = halves[first + step]
            weights = jnp.concatenate([both, both], axis=0)
            got = jnp.dot(columns[codes[0, first + step]], weights, preferred_element_type=jnp.float32)
            products.append(got[:, :W] + got[:, W:])
        for step in range(GROUP):
            place = codes[1, first + step]
            totals[place] = totals[place] + products[step]
        return carry

    lax.fori_loop(0, (codes[2, 0] + GROUP - 1) // GROUP, one_group, 0)
    me = lax.axis_index("pair")

    def give(chunk, carry):
        device = lax.bitwise_xor(me, lax.rem(chunk, far) * NEAR + chunk // far)
        for tile in range(out_tiles):
            result[device, tile * rows : (tile + 1) * rows, :] = totals[tile, pl.ds(chunk * rows, rows), :]
        return carry

    lax.fori_loop(0, chunk_count, give, 0, unroll=min(chunk_count, 16))


def local_terms(codes, blocks, halves, rows, out_tiles):
    owners, chunk_count, chunk_rows, _ = blocks.shape
    total_rows = chunk_count * rows
    in_local = chunk_rows // rows
    return pl.pallas_call(
        ladder_kernel,
        out_shape=jax.ShapeDtypeStruct((chunk_count, out_tiles * rows, W), jnp.float32),
        in_specs=[SMEM, VMEM, VMEM],
        out_specs=VMEM,
        scratch_shapes=[
            pltpu.VMEM((owners * in_local, total_rows, 2 * W), jnp.bfloat16),
            pltpu.VMEM((in_local, total_rows, W), jnp.float32),
            pltpu.VMEM((out_tiles + 1, total_rows, W), jnp.float32),
        ],
        compiler_params=pltpu.CompilerParams(vmem_limit_bytes=32 * 1024 * 1024),
    )(codes, blocks, halves)


def from_partners(value, pairs, virts, masks):
    received = []
    for mask in masks:
        routes = [(a * virts + b, (a ^ mask) * virts + (b ^ 1)) for a in range(pairs) for b in range(virts)]
        received.append(lax.ppermute(value, ("pair", "virt"), routes))
    return received


def shards(t2_amplitudes, integral_tiles, out_tiles, in_tiles, tile_counts):
    rows, columns = t2_amplitudes.shape
    local_tiles = columns // W
    slots = integral_tiles.shape[2]
    pairs, virts = lax.axis_size("pair"), lax.axis_size("virt")
    mine = t2_amplitudes.reshape(rows, local_tiles, W).transpose(1, 0, 2).reshape(local_tiles * rows, W)
    halves, codes, own = prepare(
        integral_tiles.reshape(slots, W, W),
        in_tiles.reshape(1, slots),
        out_tiles.reshape(1, slots),
        tile_counts,
        mine,
        local_tiles,
    )
    line = jnp.stack([own] + from_partners(mine, pairs, virts, range(NEAR, pairs, NEAR)))
    gathered = jnp.concatenate([line] + from_partners(line, pairs, virts, range(1, NEAR)))
    blocks = lax.all_gather(gathered, "virt", axis=0)
    partial_sums = local_terms(codes, blocks, halves, rows, local_tiles)
    received = lax.all_to_all(partial_sums, "pair", 0, 0)
    summed = jnp.sum(received, axis=0)
    return summed.reshape(local_tiles, rows, W).transpose(1, 0, 2).reshape(rows, columns)


def solution(mesh):
    return jax.shard_map(
        shards,
        mesh=mesh,
        in_specs=(
            P("pair", "virt"),
            P("pair", "virt", None, None, None),
            P("pair", "virt", None),
            P("pair", "virt", None),
            P("pair", "virt"),
        ),
        out_specs=P("pair", "virt"),
        check_vma=False,
    )
```

profile of v0, /device:TPU:0, one launch (start us, length us, event | category | flops | bytes accessed | tf_op | source)
XLA Modules:
  0.0 35.1 jit_solution(193669118979192266)
XLA Ops:
  0.0 4.5 %collective-permute-start.2 = (f32[32,128]{1,0:T(8,128)}, f32[32,128]{1,0:T(8,128)S(1)}, u32[]{:S(2)}, u32[]{:S(2)}) collective-permute-start(f32[32,128]{1,0:T(8,128)} %bitcast.28), channel_id=1, source_target_pairs={{0,25},{1,24},{2,27},{3,26},{4,29},{5,28},{6,31},{7,30},{8,17},{9,... | collective-permute-start | bytes 49160 | tf_op jit(solution)/shard_map/ppermute | solution.py:157
  4.5 0.0 collective-permute-start.1
  4.5 0.8 %collective-permute-start = (f32[32,128]{1,0:T(8,128)}, f32[32,128]{1,0:T(8,128)S(1)}, u32[]{:S(2)}, u32[]{:S(2)}) collective-permute-start(f32[32,128]{1,0:T(8,128)} %bitcast.30), channel_id=1, source_target_pairs={{0,9},{1,8},{2,11},{3,10},{4,13},{5,12},{6,15},{7,14},{8,1},{9,0},... | collective-permute-start | bytes 49160 | tf_op jit(solution)/shard_map/ppermute | solution.py:157
  6.0 1.2 %shard_map.55 = (bf16[32,128,256]{2,1,0:T(8,128)(2,1)S(1)}, s32[3,32]{1,0:T(4,128)S(1)}, f32[32,128]{1,0:T(8,128)S(1)}) custom-call(s32[1,1]{1,0:T(1,128)S(6)} %copy.15.refs_0_, s32[1,32]{1,0:T(1,128)} %bitcast.32, s32[1,32]{1,0:T(1,128)} %bitcast.33, f32[32,128,128]{2,1,0:T(8,128)} %bitcast.24, f32[32,128]{1,0:T(8,128)} %bitcast.31), custom_call_target="tpu_custom_call" | custom-call | flops 2097152 | bytes 4194304 | tf_op jit(solution)/shard_map/pallas_call | solution.py:64
  7.2 0.0 collective-permute-done.2
  7.3 1.6 %collective-permute-done.1 = f32[32,128]{1,0:T(8,128)S(1)} collective-permute-done((f32[32,128]{1,0:T(8,128)}, f32[32,128]{1,0:T(8,128)S(1)}, u32[]{:S(2)}, u32[]{:S(2)}) %collective-permute-start.1) | collective-permute-done | bytes 16416 | tf_op jit(solution)/shard_map/ppermute | solution.py:157
  8.9 0.0 collective-permute-done
  8.9 2.7 %collective-permute-start.5 = (f32[4,32,128]{2,1,0:T(8,128)S(1)}, f32[4,32,128]{2,1,0:T(8,128)S(1)}, u32[]{:S(2)}, u32[]{:S(2)}) collective-permute-start(f32[4,32,128]{2,1,0:T(8,128)S(1)} %pad_maximum_fusion), channel_id=1, source_target_pairs={{0,7},{1,6},{2,5},{3,4},{4,3},{5,2},{6,1},{7,0},{8,15},{9,14},{10,... | collective-permute-start | bytes 196616 | tf_op jit(solution)/shard_map/ppermute | solution.py:157
  11.6 0.1 collective-permute-start.4
  11.6 0.7 %collective-permute-start.3 = (f32[4,32,128]{2,1,0:T(8,128)S(1)}, f32[4,32,128]{2,1,0:T(8,128)S(1)}, u32[]{:S(2)}, u32[]{:S(2)}) collective-permute-start(f32[4,32,128]{2,1,0:T(8,128)S(1)} %pad_maximum_fusion), channel_id=1, source_target_pairs={{0,3},{1,2},{2,1},{3,0},{4,7},{5,6},{6,5},{7,4},{8,11},{9,10},{10,... | collective-permute-start | bytes 196616 | tf_op jit(solution)/shard_map/ppermute | solution.py:157
  12.3 3.0 %collective-permute-done.3 = f32[4,32,128]{2,1,0:T(8,128)S(1)} collective-permute-done((f32[4,32,128]{2,1,0:T(8,128)S(1)}, f32[4,32,128]{2,1,0:T(8,128)S(1)}, u32[]{:S(2)}, u32[]{:S(2)}) %collective-permute-start.3) | collective-permute-done | bytes 65568 | tf_op jit(solution)/shard_map/ppermute | solution.py:157
  15.3 0.5 %collective-permute-done.4 = f32[4,32,128]{2,1,0:T(8,128)S(1)} collective-permute-done((f32[4,32,128]{2,1,0:T(8,128)S(1)}, f32[4,32,128]{2,1,0:T(8,128)S(1)}, u32[]{:S(2)}, u32[]{:S(2)}) %collective-permute-start.4) | collective-permute-done | bytes 65568 | tf_op jit(solution)/shard_map/ppermute | solution.py:157
  15.8 0.0 collective-permute-done.5
  15.8 2.2 %all-gather = f32[32,32,128]{2,1,0:T(8,128)S(1)} all-gather(f32[16,32,128]{2,1,0:T(8,128)S(1)} %constant_dynamic-update-slice_fusion), channel_id=2, replica_groups=mesh['pair'=16,'virt'=2] {'virt'}, dimensions={0}, use_global_device_ids=true | all-gather | bytes 786432 | tf_op jit(solution)/shard_map/all_gather | solution.py:177
  18.0 1.1 %shard_map.56 = f32[16,32,128]{2,1,0:T(8,128)S(1)} custom-call(s32[3,32]{1,0:T(4,128)S(1)} %get-tuple-element.8.codes, f32[2,16,32,128]{3,2,1,0:T(8,128)S(1)} %bitcast.22, bf16[32,128,256]{2,1,0:T(8,128)(2,1)S(1)} %get-tuple-element.10.halves), custom_call_target="tpu_custom_call" | custom-call | tf_op jit(solution)/shard_map/pallas_call | solution.py:139
  19.1 15.3 %all_to_all.5 = f32[16,32,128]{2,1,0:T(8,128)S(1)} all-to-all(f32[16,32,128]{2,1,0:T(8,128)S(1)} %shard_map.56), channel_id=1, replica_groups=mesh['pair'=16,'virt'=2] {'pair'}, dimensions={0} | all-to-all | bytes 524288 | tf_op jit(solution)/shard_map/all_to_all | solution.py:179
  34.5 0.6 %reduce_sum.9 = f32[32,128]{1,0:T(8,128)} reduce(f32[16,32,128]{2,1,0:T(8,128)S(1)} %all_to_all.5, f32[]{:T(128)} %constant.0.clone.1), dimensions={0}, to_apply=%region_0.0 | reduce | flops 61440 | bytes 278532 | tf_op jit(solution)/shard_map/reduce_sum | solution.py:180
  (8 shorter events, 0.0 us)
Async XLA Ops:
  0.0 7.2 %collective-permute-start.2 = (f32[32,128]{1,0:T(8,128)}, f32[32,128]{1,0:T(8,128)S(1)}, u32[]{:S(2)}, u32[]{:S(2)}) collective-permute-start(f32[32,128]{1,0:T(8,128)} %bitcast.28), channel_id=1, source_target_pairs={{0,25},{1,24},{2,27},{3,26},{4,29},{5,28},{6,31},{7,30},{8,17},{9,... | collective-permute-start | bytes 49160 | tf_op jit(solution)/shard_map/ppermute | solution.py:157
  4.5 4.4 %collective-permute-start.1 = (f32[32,128]{1,0:T(8,128)}, f32[32,128]{1,0:T(8,128)S(1)}, u32[]{:S(2)}, u32[]{:S(2)}) collective-permute-start(f32[32,128]{1,0:T(8,128)} %bitcast.29), channel_id=1, source_target_pairs={{0,17},{1,16},{2,19},{3,18},{4,21},{5,20},{6,23},{7,22},{8,25},{9,... | collective-permute-start | bytes 49160 | tf_op jit(solution)/shard_map/ppermute | solution.py:157
  4.5 4.4 %collective-permute-start = (f32[32,128]{1,0:T(8,128)}, f32[32,128]{1,0:T(8,128)S(1)}, u32[]{:S(2)}, u32[]{:S(2)}) collective-permute-start(f32[32,128]{1,0:T(8,128)} %bitcast.30), channel_id=1, source_target_pairs={{0,9},{1,8},{2,11},{3,10},{4,13},{5,12},{6,15},{7,14},{8,1},{9,0},... | collective-permute-start | bytes 49160 | tf_op jit(solution)/shard_map/ppermute | solution.py:157
  8.9 6.9 %collective-permute-start.5 = (f32[4,32,128]{2,1,0:T(8,128)S(1)}, f32[4,32,128]{2,1,0:T(8,128)S(1)}, u32[]{:S(2)}, u32[]{:S(2)}) collective-permute-start(f32[4,32,128]{2,1,0:T(8,128)S(1)} %pad_maximum_fusion), channel_id=1, source_target_pairs={{0,7},{1,6},{2,5},{3,4},{4,3},{5,2},{6,1},{7,0},{8,15},{9,14},{10,... | collective-permute-start | bytes 196616 | tf_op jit(solution)/shard_map/ppermute | solution.py:157
  11.6 4.3 %collective-permute-start.4 = (f32[4,32,128]{2,1,0:T(8,128)S(1)}, f32[4,32,128]{2,1,0:T(8,128)S(1)}, u32[]{:S(2)}, u32[]{:S(2)}) collective-permute-start(f32[4,32,128]{2,1,0:T(8,128)S(1)} %pad_maximum_fusion), channel_id=1, source_target_pairs={{0,5},{1,4},{2,7},{3,6},{4,1},{5,0},{6,3},{7,2},{8,13},{9,12},{10,... | collective-permute-start | bytes 196616 | tf_op jit(solution)/shard_map/ppermute | solution.py:157
  11.6 3.7 %collective-permute-start.3 = (f32[4,32,128]{2,1,0:T(8,128)S(1)}, f32[4,32,128]{2,1,0:T(8,128)S(1)}, u32[]{:S(2)}, u32[]{:S(2)}) collective-permute-start(f32[4,32,128]{2,1,0:T(8,128)S(1)} %pad_maximum_fusion), channel_id=1, source_target_pairs={{0,3},{1,2},{2,1},{3,0},{4,7},{5,6},{6,5},{7,4},{8,11},{9,10},{10,... | collective-permute-start | bytes 196616 | tf_op jit(solution)/shard_map/ppermute | solution.py:157
where the time goes:
time: 35.1 us
  blocking collectives  17.5 us (50%)
  starting transfers between devices  8.77 us (25%)
  waiting for transfers between devices  5.11 us (15%)
  Pallas kernels  2.34 us (7%)
  between operations  0.71 us (2%)
  other arithmetic  0.63 us (2%)
    all_to_all x1, blocking collectives, shards(): received = lax.all_to_all(partial_sums, 'pair', 0, 0)  15.3 us
    ppermute x6, starting transfers between devices, from_partners(): received.append(lax.ppermute(value, ('pair', 'virt'), routes))  8.77 us
    ppermute x6, waiting for transfers between devices, from_partners(): received.append(lax.ppermute(value, ('pair', 'virt'), routes))  5.11 us
    all_gather x1, blocking collectives, shards(): blocks = lax.all_gather(gathered, 'virt', axis=0)  2.18 us
    pallas_call x1, Pallas kernels, prepare(): pl.pallas_call(kernel, out_shape=(jax.ShapeDtypeStruct((slots, W, 2 * W),...  1.24 us
    pallas_call x1, Pallas kernels, local_terms(): pl.pallas_call(ladder_kernel, out_shape=jax.ShapeDtypeStruct((chunk_count...  1.1 us
  transfers between devices with their start and end apart: 6, of which 3 were waited for; matrix products, arithmetic and copies ran while one was open for 0% of the time, Pallas kernels for 4%

commit v1 on v0

--- a/solution.py
+++ b/solution.py
@@ -84,7 +84,7 @@
 def ladder_kernel(codes, blocks, halves, result, columns, flat, totals):
     owners, chunk_count = blocks.shape[:2]
     out_tiles = totals.shape[0] - 1
-    rows = result.shape[1] // out_tiles
+    rows = result.shape[2] // out_tiles
     in_local = blocks.shape[2] // rows
     totals[...] = jnp.zeros_like(totals)
 
@@ -121,12 +121,15 @@
         return carry
 
     lax.fori_loop(0, (codes[2, 0] + GROUP - 1) // GROUP, one_group, 0)
-    me = lax.axis_index("pair")
+    turned = lax.rem(lax.axis_index("virt"), 2) == 1
 
     def give(chunk, carry):
-        device = lax.bitwise_xor(me, lax.rem(chunk, far) * NEAR + chunk // far)
+        a, b = chunk // far, lax.rem(chunk, far)
+        low, next_low = lax.rem(a, 2), a // 2
+        side = jnp.where(turned, next_low, low)
+        place = b * (NEAR // 2) + jnp.where(turned, low, next_low)
         for tile in range(out_tiles):
-            result[device, tile * rows : (tile + 1) * rows, :] = totals[tile, pl.ds(chunk * rows, rows), :]
+            result[side, place, tile * rows : (tile + 1) * rows, :] = totals[tile, pl.ds(chunk * rows, rows), :]
         return carry
 
     lax.fori_loop(0, chunk_count, give, 0, unroll=min(chunk_count, 16))
@@ -138,7 +141,7 @@
     in_local = chunk_rows // rows
     return pl.pallas_call(
         ladder_kernel,
-        out_shape=jax.ShapeDtypeStruct((chunk_count, out_tiles * rows, W), jnp.float32),
+        out_shape=jax.ShapeDtypeStruct((2, chunk_count // 2, out_tiles * rows, W), jnp.float32),
         in_specs=[SMEM, VMEM, VMEM],
         out_specs=VMEM,
         scratch_shapes=[
@@ -156,6 +159,37 @@
         routes = [(a * virts + b, (a ^ mask) * virts + (b ^ 1)) for a in range(pairs) for b in range(virts)]
         received.append(lax.ppermute(value, ("pair", "virt"), routes))
     return received
+
+
+def distance(place, side, b):
+    mask = 2 * place + side
+    return mask if b % 2 == 0 else mask & ~3 | (mask & 1) << 1 | (mask & 2) >> 1
+
+
+def exchange_routes(pairs, virts):
+    return [(a * virts + b, (a ^ distance(0, 1, b)) * virts + b) for a in range(pairs) for b in range(virts)]
+
+
+def one_way_routes(pairs, virts, place, half):
+    return [
+        (a * virts + b, (a ^ distance(place, 1, b)) * virts + b)
+        for a in range(pairs)
+        for b in range(virts)
+        if ((a & distance(0, 1, b)) != 0) == half
+    ]
+
+
+def scatter_sum(parts, pairs, virts):
+    axes = ("pair", "virt")
+    held = parts[1] + lax.ppermute(parts[0], axes, exchange_routes(pairs, virts))
+    received = []
+    for half in (False, True):
+        if half:
+            held, received[0] = lax.optimization_barrier((held, received[0]))
+        received += [
+            lax.ppermute(held[place], axes, one_way_routes(pairs, virts, place, half)) for place in range(pairs // 2)
+        ]
+    return sum(received[1:], received[0])
 
 
 def shards(t2_amplitudes, integral_tiles, out_tiles, in_tiles, tile_counts):
@@ -176,8 +210,7 @@
     gathered = jnp.concatenate([line] + from_partners(line, pairs, virts, range(1, NEAR)))
     blocks = lax.all_gather(gathered, "virt", axis=0)
     partial_sums = local_terms(codes, blocks, halves, rows, local_tiles)
-    received = lax.all_to_all(partial_sums, "pair", 0, 0)
-    summed = jnp.sum(received, axis=0)
+    summed = scatter_sum(partial_sums, pairs, virts)
     return summed.reshape(local_tiles, rows, W).transpose(1, 0, 2).reshape(rows, columns)
 
 

time: 35.1 us -> 58.3 us (1.66)
  starting transfers between devices: 8.77 us -> 35 us
  blocking collectives: 17.5 us -> 2.18 us
  waiting for transfers between devices: 5.11 us -> 16.7 us
    ppermute x0 -> x17, starting transfers between devices: none -> 26.2 us  [the longest x16 24.8 us: scatter_sum(): lax.ppermute(held[place], axes, one_way_routes(pairs, virts, place, half))]
    all_to_all x1 -> x0, blocking collectives: 15.3 us -> none  [shards(): received = lax.all_to_all(partial_sums, 'pair', 0, 0)]
    ppermute x0 -> x17, waiting for transfers between devices: none -> 11.6 us  [the longest x16 7.93 us: scatter_sum(): lax.ppermute(held[place], axes, one_way_routes(pairs, virts, place, half))]
    add x0 -> x2, other arithmetic: none -> 0.64 us  [the longest x1 0.63 us: scatter_sum(): return sum(received[1:], received[0])]
    reduce_sum x1 -> x0, other arithmetic: 0.63 us -> none  [shards(): summed = jnp.sum(received, axis=0)]
  transfers between devices with their start and end apart: 6 -> 23, of which waited for: 3 -> 9; matrix products, arithmetic and copies ran while one was open for 0% -> 0% of each run, Pallas kernels for 4% -> 2%
where the time goes in v1:
time: 58.3 us; the launch traced here: 57.8 us
  starting transfers between devices  35 us (60%)
  waiting for transfers between devices  16.7 us (29%)
  Pallas kernels  2.34 us (4%)
  blocking collectives  2.18 us (4%)
  between operations  0.95 us (2%)
  other arithmetic  0.65 us (1%)
    ppermute x16, starting transfers between devices, scatter_sum(): lax.ppermute(held[place], axes, one_way_routes(pairs, virts, place, half))  24.8 us
    ppermute x6, starting transfers between devices, from_partners(): received.append(lax.ppermute(value, ('pair', 'virt'), routes))  8.77 us
    ppermute x16, waiting for transfers between devices, scatter_sum(): lax.ppermute(held[place], axes, one_way_routes(pairs, virts, place, half))  7.93 us
    ppermute x6, waiting for transfers between devices, from_partners(): received.append(lax.ppermute(value, ('pair', 'virt'), routes))  5.11 us
    ppermute x1, waiting for transfers between devices, scatter_sum(): lax.ppermute(parts[0], axes, exchange_routes(pairs, virts))  3.62 us
    all_gather x1, blocking collectives, shards(): blocks = lax.all_gather(gathered, 'virt', axis=0)  2.18 us
    ppermute x1, starting transfers between devices, scatter_sum(): lax.ppermute(parts[0], axes, exchange_routes(pairs, virts))  1.42 us
    pallas_call x1, Pallas kernels, prepare(): pl.pallas_call(kernel, out_shape=(jax.ShapeDtypeStruct((slots, W, 2 * W),...  1.24 us
  transfers between devices with their start and end apart: 23, of which 9 were waited for; matrix products, arithmetic and copies ran while one was open for 0% of the time, Pallas kernels for 2%

profile of v1, /device:TPU:0, one launch (start us, length us, event | category | flops | bytes accessed | tf_op | source)
XLA Modules:
  0.0 57.8 jit_solution(6193913813913670825)
XLA Ops:
  0.0 4.5 %collective-permute-start.2 = (f32[32,128]{1,0:T(8,128)}, f32[32,128]{1,0:T(8,128)S(1)}, u32[]{:S(2)}, u32[]{:S(2)}) collective-permute-start(f32[32,128]{1,0:T(8,128)} %bitcast.66), channel_id=1, source_target_pairs={{0,25},{1,24},{2,27},{3,26},{4,29},{5,28},{6,31},{7,30},{8,17},{9,... | collective-permute-start | bytes 49160 | tf_op jit(solution)/shard_map/ppermute | solution.py:160
  4.5 0.0 collective-permute-start.1
  4.5 0.8 %collective-permute-start = (f32[32,128]{1,0:T(8,128)}, f32[32,128]{1,0:T(8,128)S(1)}, u32[]{:S(2)}, u32[]{:S(2)}) collective-permute-start(f32[32,128]{1,0:T(8,128)} %bitcast.68), channel_id=1, source_target_pairs={{0,9},{1,8},{2,11},{3,10},{4,13},{5,12},{6,15},{7,14},{8,1},{9,0},... | collective-permute-start | bytes 49160 | tf_op jit(solution)/shard_map/ppermute | solution.py:160
  6.0 1.2 %shard_map.55 = (bf16[32,128,256]{2,1,0:T(8,128)(2,1)S(1)}, s32[3,32]{1,0:T(4,128)S(1)}, f32[32,128]{1,0:T(8,128)S(1)}) custom-call(s32[1,1]{1,0:T(1,128)S(6)} %copy.16.refs_0_, s32[1,32]{1,0:T(1,128)} %bitcast.70, s32[1,32]{1,0:T(1,128)} %bitcast.71, f32[32,128,128]{2,1,0:T(8,128)} %bitcast.62, f32[32,128]{1,0:T(8,128)} %bitcast.69), custom_call_target="tpu_custom_call" | custom-call | flops 2097152 | bytes 4194304 | tf_op jit(solution)/shard_map/pallas_call | solution.py:64
  7.2 0.0 collective-permute-done.2
  7.3 1.6 %collective-permute-done.1 = f32[32,128]{1,0:T(8,128)S(1)} collective-permute-done((f32[32,128]{1,0:T(8,128)}, f32[32,128]{1,0:T(8,128)S(1)}, u32[]{:S(2)}, u32[]{:S(2)}) %collective-permute-start.1) | collective-permute-done | bytes 16416 | tf_op jit(solution)/shard_map/ppermute | solution.py:160
  8.9 0.0 collective-permute-done
  8.9 2.7 %collective-permute-start.5 = (f32[4,32,128]{2,1,0:T(8,128)S(1)}, f32[4,32,128]{2,1,0:T(8,128)S(1)}, u32[]{:S(2)}, u32[]{:S(2)}) collective-permute-start(f32[4,32,128]{2,1,0:T(8,128)S(1)} %pad_maximum_fusion), channel_id=1, source_target_pairs={{0,7},{1,6},{2,5},{3,4},{4,3},{5,2},{6,1},{7,0},{8,15},{9,14},{10,... | collective-permute-start | bytes 196616 | tf_op jit(solution)/shard_map/ppermute | solution.py:160
  11.6 0.1 collective-permute-start.4
  11.6 0.7 %collective-permute-start.3 = (f32[4,32,128]{2,1,0:T(8,128)S(1)}, f32[4,32,128]{2,1,0:T(8,128)S(1)}, u32[]{:S(2)}, u32[]{:S(2)}) collective-permute-start(f32[4,32,128]{2,1,0:T(8,128)S(1)} %pad_maximum_fusion), channel_id=1, source_target_pairs={{0,3},{1,2},{2,1},{3,0},{4,7},{5,6},{6,5},{7,4},{8,11},{9,10},{10,... | collective-permute-start | bytes 196616 | tf_op jit(solution)/shard_map/ppermute | solution.py:160
  12.3 3.0 %collective-permute-done.3 = f32[4,32,128]{2,1,0:T(8,128)S(1)} collective-permute-done((f32[4,32,128]{2,1,0:T(8,128)S(1)}, f32[4,32,128]{2,1,0:T(8,128)S(1)}, u32[]{:S(2)}, u32[]{:S(2)}) %collective-permute-start.3) | collective-permute-done | bytes 65568 | tf_op jit(solution)/shard_map/ppermute | solution.py:160
  15.3 0.5 collective-permute-done.4
  15.8 0.0 collective-permute-done.5
  15.8 2.2 %all-gather = f32[32,32,128]{2,1,0:T(8,128)S(1)} all-gather(f32[16,32,128]{2,1,0:T(8,128)S(1)} %constant_dynamic-update-slice_fusion), channel_id=2, replica_groups=mesh['pair'=16,'virt'=2] {'virt'}, dimensions={0}, use_global_device_ids=true | all-gather | bytes 786432 | tf_op jit(solution)/shard_map/all_gather | solution.py:211
  18.0 1.1 %shard_map.56 = f32[2,8,32,128]{3,2,1,0:T(8,128)S(1)} custom-call(s32[3,32]{1,0:T(4,128)S(1)} %get-tuple-element.10.codes, f32[2,16,32,128]{3,2,1,0:T(8,128)S(1)} %bitcast.60, bf16[32,128,256]{2,1,0:T(8,128)(2,1)S(1)} %get-tuple-element.12.halves), custom_call_target="tpu_custom_call" | custom-call | tf_op jit(solution)/shard_map/pallas_call | solution.py:142
  19.2 1.4 %collective-permute-start.6 = (f32[8,32,128]{2,1,0:T(8,128)S(1)}, f32[8,32,128]{2,1,0:T(8,128)S(1)}, u32[]{:S(2)}, u32[]{:S(2)}) collective-permute-start(f32[8,32,128]{2,1,0:T(8,128)S(1)} %slice_bitcast_fusion), channel_id=1, source_target_pairs={{0,2},{1,5},{2,0},{3,7},{4,6},{5,1},{6,4},{7,3},{8,10},{9,13},{10,... | collective-permute-start | bytes 393224 | tf_op jit(solution)/shard_map/ppermute | solution.py:184
  20.6 3.6 %collective-permute-done.6 = f32[8,32,128]{2,1,0:T(8,128)S(1)} collective-permute-done((f32[8,32,128]{2,1,0:T(8,128)S(1)}, f32[8,32,128]{2,1,0:T(8,128)S(1)}, u32[]{:S(2)}, u32[]{:S(2)}) %collective-permute-start.6) | collective-permute-done | bytes 131104 | tf_op jit(solution)/shard_map/ppermute | solution.py:184
  24.2 3.3 %collective-permute-start.7 = (f32[32,128]{1,0:T(8,128)S(1)}, f32[32,128]{1,0:T(8,128)S(1)}, u32[]{:S(2)}, u32[]{:S(2)}) collective-permute-start(f32[32,128]{1,0:T(8,128)S(1)} %get-tuple-element.22), channel_id=1, source_target_pairs={{0,2},{1,5},{3,7},{4,6},{8,10},{9,13},{11,15},{12,14},{16,18},{17,... | collective-permute-start | bytes 49160 | tf_op jit(solution)/shard_map/ppermute | solution.py:190
  27.5 1.8 %collective-permute-start.8 = (f32[32,128]{1,0:T(8,128)S(1)}, f32[32,128]{1,0:T(8,128)S(1)}, u32[]{:S(2)}, u32[]{:S(2)}) collective-permute-start(f32[32,128]{1,0:T(8,128)S(1)} %get-tuple-element.15), channel_id=1, source_target_pairs={{0,6},{1,7},{3,5},{4,2},{8,14},{9,15},{11,13},{12,10},{16,22},{17,... | collective-permute-start | bytes 49160 | tf_op jit(solution)/shard_map/ppermute | solution.py:190
  29.3 2.7 %collective-permute-start.14 = (f32[32,128]{1,0:T(8,128)S(1)}, f32[32,128]{1,0:T(8,128)S(1)}, u32[]{:S(2)}, u32[]{:S(2)}) collective-permute-start(f32[32,128]{1,0:T(8,128)S(1)} %get-tuple-element.16), channel_id=1, source_target_pairs={{0,30},{1,31},{3,29},{4,26},{8,22},{9,23},{11,21},{12,18},{16,14},... | collective-permute-start | bytes 49160 | tf_op jit(solution)/shard_map/ppermute | solution.py:190
  32.0 1.3 %collective-permute-start.13 = (f32[32,128]{1,0:T(8,128)S(1)}, f32[32,128]{1,0:T(8,128)S(1)}, u32[]{:S(2)}, u32[]{:S(2)}) collective-permute-start(f32[32,128]{1,0:T(8,128)S(1)} %get-tuple-element.17), channel_id=1, source_target_pairs={{0,26},{1,29},{3,31},{4,30},{8,18},{9,21},{11,23},{12,22},{16,10},... | collective-permute-start | bytes 49160 | tf_op jit(solution)/shard_map/ppermute | solution.py:190
  33.3 1.6 %collective-permute-start.12 = (f32[32,128]{1,0:T(8,128)S(1)}, f32[32,128]{1,0:T(8,128)S(1)}, u32[]{:S(2)}, u32[]{:S(2)}) collective-permute-start(f32[32,128]{1,0:T(8,128)S(1)} %get-tuple-element.18), channel_id=1, source_target_pairs={{0,22},{1,23},{3,21},{4,18},{8,30},{9,31},{11,29},{12,26},{16,6},{... | collective-permute-start | bytes 49160 | tf_op jit(solution)/shard_map/ppermute | solution.py:190
  34.9 0.0 collective-permute-done.7
  34.9 1.3 %collective-permute-start.11 = (f32[32,128]{1,0:T(8,128)S(1)}, f32[32,128]{1,0:T(8,128)S(1)}, u32[]{:S(2)}, u32[]{:S(2)}) collective-permute-start(f32[32,128]{1,0:T(8,128)S(1)} %get-tuple-element.19), channel_id=1, source_target_pairs={{0,18},{1,21},{3,23},{4,22},{8,26},{9,29},{11,31},{12,30},{16,2},{... | collective-permute-start | bytes 49160 | tf_op jit(solution)/shard_map/ppermute | solution.py:190
  36.2 0.0 collective-permute-done.8
  36.2 1.3 %collective-permute-start.10 = (f32[32,128]{1,0:T(8,128)S(1)}, f32[32,128]{1,0:T(8,128)S(1)}, u32[]{:S(2)}, u32[]{:S(2)}) collective-permute-start(f32[32,128]{1,0:T(8,128)S(1)} %get-tuple-element.20), channel_id=1, source_target_pairs={{0,14},{1,15},{3,13},{4,10},{8,6},{9,7},{11,5},{12,2},{16,30},{17,... | collective-permute-start | bytes 49160 | tf_op jit(solution)/shard_map/ppermute | solution.py:190
  37.5 0.0 collective-permute-done.14
  37.5 1.3 %collective-permute-start.9 = (f32[32,128]{1,0:T(8,128)S(1)}, f32[32,128]{1,0:T(8,128)S(1)}, u32[]{:S(2)}, u32[]{:S(2)}) collective-permute-start(f32[32,128]{1,0:T(8,128)S(1)} %get-tuple-element.21), channel_id=1, source_target_pairs={{0,10},{1,13},{3,15},{4,14},{8,2},{9,5},{11,7},{12,6},{16,26},{17,... | collective-permute-start | bytes 49160 | tf_op jit(solution)/shard_map/ppermute | solution.py:190
  38.8 0.0 collective-permute-done.13
  38.8 1.3 %collective-permute-start.15 = (f32[32,128]{1,0:T(8,128)S(1)}, f32[32,128]{1,0:T(8,128)S(1)}, u32[]{:S(2)}, u32[]{:S(2)}) collective-permute-start(f32[32,128]{1,0:T(8,128)S(1)} %get-tuple-element.23), channel_id=1, source_target_pairs={{2,0},{5,1},{6,4},{7,3},{10,8},{13,9},{14,12},{15,11},{18,16},{21,... | collective-permute-start | bytes 49160 | tf_op jit(solution)/shard_map/ppermute | solution.py:190
  40.1 0.0 collective-permute-done.12
  40.1 1.3 %collective-permute-start.22 = (f32[32,128]{1,0:T(8,128)S(1)}, f32[32,128]{1,0:T(8,128)S(1)}, u32[]{:S(2)}, u32[]{:S(2)}) collective-permute-start(f32[32,128]{1,0:T(8,128)S(1)} %get-tuple-element.24), channel_id=1, source_target_pairs={{2,28},{5,27},{6,24},{7,25},{10,20},{13,19},{14,16},{15,17},{18,12... | collective-permute-start | bytes 49160 | tf_op jit(solution)/shard_map/ppermute | solution.py:190
  41.4 0.0 collective-permute-done.11
  41.4 1.3 %collective-permute-start.21 = (f32[32,128]{1,0:T(8,128)S(1)}, f32[32,128]{1,0:T(8,128)S(1)}, u32[]{:S(2)}, u32[]{:S(2)}) collective-permute-start(f32[32,128]{1,0:T(8,128)S(1)} %get-tuple-element.25), channel_id=1, source_target_pairs={{2,24},{5,25},{6,28},{7,27},{10,16},{13,17},{14,20},{15,19},{18,8}... | collective-permute-start | bytes 49160 | tf_op jit(solution)/shard_map/ppermute | solution.py:190
  42.7 0.0 collective-permute-done.10
  42.7 1.3 %collective-permute-start.20 = (f32[32,128]{1,0:T(8,128)S(1)}, f32[32,128]{1,0:T(8,128)S(1)}, u32[]{:S(2)}, u32[]{:S(2)}) collective-permute-start(f32[32,128]{1,0:T(8,128)S(1)} %get-tuple-element.26), channel_id=1, source_target_pairs={{2,20},{5,19},{6,16},{7,17},{10,28},{13,27},{14,24},{15,25},{18,4}... | collective-permute-start | bytes 49160 | tf_op jit(solution)/shard_map/ppermute | solution.py:190
  44.0 0.0 collective-permute-done.9
  44.1 1.3 %collective-permute-start.19 = (f32[32,128]{1,0:T(8,128)S(1)}, f32[32,128]{1,0:T(8,128)S(1)}, u32[]{:S(2)}, u32[]{:S(2)}) collective-permute-start(f32[32,128]{1,0:T(8,128)S(1)} %get-tuple-element.27), channel_id=1, source_target_pairs={{2,16},{5,17},{6,20},{7,19},{10,24},{13,25},{14,28},{15,27},{18,0}... | collective-permute-start | bytes 49160 | tf_op jit(solution)/shard_map/ppermute | solution.py:190
  45.4 0.0 collective-permute-done.15
  45.4 1.3 %collective-permute-start.18 = (f32[32,128]{1,0:T(8,128)S(1)}, f32[32,128]{1,0:T(8,128)S(1)}, u32[]{:S(2)}, u32[]{:S(2)}) collective-permute-start(f32[32,128]{1,0:T(8,128)S(1)} %get-tuple-element.28), channel_id=1, source_target_pairs={{2,12},{5,11},{6,8},{7,9},{10,4},{13,3},{14,0},{15,1},{18,28},{21,... | collective-permute-start | bytes 49160 | tf_op jit(solution)/shard_map/ppermute | solution.py:190
  46.7 2.7 %collective-permute-done.22 = f32[32,128]{1,0:T(8,128)S(1)} collective-permute-done((f32[32,128]{1,0:T(8,128)S(1)}, f32[32,128]{1,0:T(8,128)S(1)}, u32[]{:S(2)}, u32[]{:S(2)}) %collective-permute-start.22) | collective-permute-done | bytes 16416 | tf_op jit(solution)/shard_map/ppermute | solution.py:190
  49.4 1.3 %collective-permute-start.17 = (f32[32,128]{1,0:T(8,128)S(1)}, f32[32,128]{1,0:T(8,128)S(1)}, u32[]{:S(2)}, u32[]{:S(2)}) collective-permute-start(f32[32,128]{1,0:T(8,128)S(1)} %get-tuple-element.29), channel_id=1, source_target_pairs={{2,8},{5,9},{6,12},{7,11},{10,0},{13,1},{14,4},{15,3},{18,24},{21,... | collective-permute-start | bytes 49160 | tf_op jit(solution)/shard_map/ppermute | solution.py:190
  50.6 0.0 collective-permute-done.21
  50.7 1.3 %collective-permute-start.16 = (f32[32,128]{1,0:T(8,128)S(1)}, f32[32,128]{1,0:T(8,128)S(1)}, u32[]{:S(2)}, u32[]{:S(2)}) collective-permute-start(f32[32,128]{1,0:T(8,128)S(1)} %get-tuple-element.30), channel_id=1, source_target_pairs={{2,4},{5,3},{6,0},{7,1},{10,12},{13,11},{14,8},{15,9},{18,20},{21,... | collective-permute-start | bytes 49160 | tf_op jit(solution)/shard_map/ppermute | solution.py:190
  52.0 0.0 collective-permute-done.20
  52.0 0.5 collective-permute-done.19
  52.5 1.5 %collective-permute-done.18 = f32[32,128]{1,0:T(8,128)S(1)} collective-permute-done((f32[32,128]{1,0:T(8,128)S(1)}, f32[32,128]{1,0:T(8,128)S(1)}, u32[]{:S(2)}, u32[]{:S(2)}) %collective-permute-start.18) | collective-permute-done | bytes 16416 | tf_op jit(solution)/shard_map/ppermute | solution.py:190
  54.0 1.9 %collective-permute-done.17 = f32[32,128]{1,0:T(8,128)S(1)} collective-permute-done((f32[32,128]{1,0:T(8,128)S(1)}, f32[32,128]{1,0:T(8,128)S(1)}, u32[]{:S(2)}, u32[]{:S(2)}) %collective-permute-start.17) | collective-permute-done | bytes 16416 | tf_op jit(solution)/shard_map/ppermute | solution.py:190
  55.9 1.3 %collective-permute-done.16 = f32[32,128]{1,0:T(8,128)S(1)} collective-permute-done((f32[32,128]{1,0:T(8,128)S(1)}, f32[32,128]{1,0:T(8,128)S(1)}, u32[]{:S(2)}, u32[]{:S(2)}) %collective-permute-start.16) | collective-permute-done | bytes 16416 | tf_op jit(solution)/shard_map/ppermute | solution.py:190
  57.2 0.6 %add_add_fusion = f32[32,128]{1,0:T(8,128)} fusion(f32[32,128]{1,0:T(8,128)S(1)} %collective-permute-done.22, f32[32,128]{1,0:T(8,128)S(1)} %collective-permute-done.21, f32[32,128]{1,0:T(8,128)S(1)} %collective-permute-done.20, f32[32,128]{1,0:T(8,128)S(1)} %collective-permute-done.19, f32[32,128]{1,0:T(8,128)S(1)} %collective-permute-done.18, ...), kind=kLoop, calls=%fused_computation.20 | loop fusion | flops 61440 | bytes 278528 | tf_op jit(solution)/shard_map/add | solution.py:192
  (12 shorter events, 0.1 us)
Async XLA Ops:
  0.0 7.2 %collective-permute-start.2 = (f32[32,128]{1,0:T(8,128)}, f32[32,128]{1,0:T(8,128)S(1)}, u32[]{:S(2)}, u32[]{:S(2)}) collective-permute-start(f32[32,128]{1,0:T(8,128)} %bitcast.66), channel_id=1, source_target_pairs={{0,25},{1,24},{2,27},{3,26},{4,29},{5,28},{6,31},{7,30},{8,17},{9,... | collective-permute-start | bytes 49160 | tf_op jit(solution)/shard_map/ppermute | solution.py:160
  4.5 4.4 %collective-permute-start.1 = (f32[32,128]{1,0:T(8,128)}, f32[32,128]{1,0:T(8,128)S(1)}, u32[]{:S(2)}, u32[]{:S(2)}) collective-permute-start(f32[32,128]{1,0:T(8,128)} %bitcast.67), channel_id=1, source_target_pairs={{0,17},{1,16},{2,19},{3,18},{4,21},{5,20},{6,23},{7,22},{8,25},{9,... | collective-permute-start | bytes 49160 | tf_op jit(solution)/shard_map/ppermute | solution.py:160
  4.5 4.4 %collective-permute-start = (f32[32,128]{1,0:T(8,128)}, f32[32,128]{1,0:T(8,128)S(1)}, u32[]{:S(2)}, u32[]{:S(2)}) collective-permute-start(f32[32,128]{1,0:T(8,128)} %bitcast.68), channel_id=1, source_target_pairs={{0,9},{1,8},{2,11},{3,10},{4,13},{5,12},{6,15},{7,14},{8,1},{9,0},... | collective-permute-start | bytes 49160 | tf_op jit(solution)/shard_map/ppermute | solution.py:160
  8.9 6.9 %collective-permute-start.5 = (f32[4,32,128]{2,1,0:T(8,128)S(1)}, f32[4,32,128]{2,1,0:T(8,128)S(1)}, u32[]{:S(2)}, u32[]{:S(2)}) collective-permute-start(f32[4,32,128]{2,1,0:T(8,128)S(1)} %pad_maximum_fusion), channel_id=1, source_target_pairs={{0,7},{1,6},{2,5},{3,4},{4,3},{5,2},{6,1},{7,0},{8,15},{9,14},{10,... | collective-permute-start | bytes 196616 | tf_op jit(solution)/shard_map/ppermute | solution.py:160
  11.6 4.3 %collective-permute-start.4 = (f32[4,32,128]{2,1,0:T(8,128)S(1)}, f32[4,32,128]{2,1,0:T(8,128)S(1)}, u32[]{:S(2)}, u32[]{:S(2)}) collective-permute-start(f32[4,32,128]{2,1,0:T(8,128)S(1)} %pad_maximum_fusion), channel_id=1, source_target_pairs={{0,5},{1,4},{2,7},{3,6},{4,1},{5,0},{6,3},{7,2},{8,13},{9,12},{10,... | collective-permute-start | bytes 196616 | tf_op jit(solution)/shard_map/ppermute | solution.py:160
  11.6 3.7 %collective-permute-start.3 = (f32[4,32,128]{2,1,0:T(8,128)S(1)}, f32[4,32,128]{2,1,0:T(8,128)S(1)}, u32[]{:S(2)}, u32[]{:S(2)}) collective-permute-start(f32[4,32,128]{2,1,0:T(8,128)S(1)} %pad_maximum_fusion), channel_id=1, source_target_pairs={{0,3},{1,2},{2,1},{3,0},{4,7},{5,6},{6,5},{7,4},{8,11},{9,10},{10,... | collective-permute-start | bytes 196616 | tf_op jit(solution)/shard_map/ppermute | solution.py:160
  19.2 5.0 %collective-permute-start.6 = (f32[8,32,128]{2,1,0:T(8,128)S(1)}, f32[8,32,128]{2,1,0:T(8,128)S(1)}, u32[]{:S(2)}, u32[]{:S(2)}) collective-permute-start(f32[8,32,128]{2,1,0:T(8,128)S(1)} %slice_bitcast_fusion), channel_id=1, source_target_pairs={{0,2},{1,5},{2,0},{3,7},{4,6},{5,1},{6,4},{7,3},{8,10},{9,13},{10,... | collective-permute-start | bytes 393224 | tf_op jit(solution)/shard_map/ppermute | solution.py:184
  24.2 10.6 %collective-permute-start.7 = (f32[32,128]{1,0:T(8,128)S(1)}, f32[32,128]{1,0:T(8,128)S(1)}, u32[]{:S(2)}, u32[]{:S(2)}) collective-permute-start(f32[32,128]{1,0:T(8,128)S(1)} %get-tuple-element.22), channel_id=1, source_target_pairs={{0,2},{1,5},{3,7},{4,6},{8,10},{9,13},{11,15},{12,14},{16,18},{17,... | collective-permute-start | bytes 49160 | tf_op jit(solution)/shard_map/ppermute | solution.py:190
  27.5 8.7 %collective-permute-start.8 = (f32[32,128]{1,0:T(8,128)S(1)}, f32[32,128]{1,0:T(8,128)S(1)}, u32[]{:S(2)}, u32[]{:S(2)}) collective-permute-start(f32[32,128]{1,0:T(8,128)S(1)} %get-tuple-element.15), channel_id=1, source_target_pairs={{0,6},{1,7},{3,5},{4,2},{8,14},{9,15},{11,13},{12,10},{16,22},{17,... | collective-permute-start | bytes 49160 | tf_op jit(solution)/shard_map/ppermute | solution.py:190
  29.3 8.2 %collective-permute-start.14 = (f32[32,128]{1,0:T(8,128)S(1)}, f32[32,128]{1,0:T(8,128)S(1)}, u32[]{:S(2)}, u32[]{:S(2)}) collective-permute-start(f32[32,128]{1,0:T(8,128)S(1)} %get-tuple-element.16), channel_id=1, source_target_pairs={{0,30},{1,31},{3,29},{4,26},{8,22},{9,23},{11,21},{12,18},{16,14},... | collective-permute-start | bytes 49160 | tf_op jit(solution)/shard_map/ppermute | solution.py:190
  32.0 6.8 %collective-permute-start.13 = (f32[32,128]{1,0:T(8,128)S(1)}, f32[32,128]{1,0:T(8,128)S(1)}, u32[]{:S(2)}, u32[]{:S(2)}) collective-permute-start(f32[32,128]{1,0:T(8,128)S(1)} %get-tuple-element.17), channel_id=1, source_target_pairs={{0,26},{1,29},{3,31},{4,30},{8,18},{9,21},{11,23},{12,22},{16,10},... | collective-permute-start | bytes 49160 | tf_op jit(solution)/shard_map/ppermute | solution.py:190
  33.3 6.9 %collective-permute-start.12 = (f32[32,128]{1,0:T(8,128)S(1)}, f32[32,128]{1,0:T(8,128)S(1)}, u32[]{:S(2)}, u32[]{:S(2)}) collective-permute-start(f32[32,128]{1,0:T(8,128)S(1)} %get-tuple-element.18), channel_id=1, source_target_pairs={{0,22},{1,23},{3,21},{4,18},{8,30},{9,31},{11,29},{12,26},{16,6},{... | collective-permute-start | bytes 49160 | tf_op jit(solution)/shard_map/ppermute | solution.py:190
  34.9 6.6 %collective-permute-start.11 = (f32[32,128]{1,0:T(8,128)S(1)}, f32[32,128]{1,0:T(8,128)S(1)}, u32[]{:S(2)}, u32[]{:S(2)}) collective-permute-start(f32[32,128]{1,0:T(8,128)S(1)} %get-tuple-element.19), channel_id=1, source_target_pairs={{0,18},{1,21},{3,23},{4,22},{8,26},{9,29},{11,31},{12,30},{16,2},{... | collective-permute-start | bytes 49160 | tf_op jit(solution)/shard_map/ppermute | solution.py:190
  36.2 6.5 %collective-permute-start.10 = (f32[32,128]{1,0:T(8,128)S(1)}, f32[32,128]{1,0:T(8,128)S(1)}, u32[]{:S(2)}, u32[]{:S(2)}) collective-permute-start(f32[32,128]{1,0:T(8,128)S(1)} %get-tuple-element.20), channel_id=1, source_target_pairs={{0,14},{1,15},{3,13},{4,10},{8,6},{9,7},{11,5},{12,2},{16,30},{17,... | collective-permute-start | bytes 49160 | tf_op jit(solution)/shard_map/ppermute | solution.py:190
  37.5 6.5 %collective-permute-start.9 = (f32[32,128]{1,0:T(8,128)S(1)}, f32[32,128]{1,0:T(8,128)S(1)}, u32[]{:S(2)}, u32[]{:S(2)}) collective-permute-start(f32[32,128]{1,0:T(8,128)S(1)} %get-tuple-element.21), channel_id=1, source_target_pairs={{0,10},{1,13},{3,15},{4,14},{8,2},{9,5},{11,7},{12,6},{16,26},{17,... | collective-permute-start | bytes 49160 | tf_op jit(solution)/shard_map/ppermute | solution.py:190
  38.8 6.5 %collective-permute-start.15 = (f32[32,128]{1,0:T(8,128)S(1)}, f32[32,128]{1,0:T(8,128)S(1)}, u32[]{:S(2)}, u32[]{:S(2)}) collective-permute-start(f32[32,128]{1,0:T(8,128)S(1)} %get-tuple-element.23), channel_id=1, source_target_pairs={{2,0},{5,1},{6,4},{7,3},{10,8},{13,9},{14,12},{15,11},{18,16},{21,... | collective-permute-start | bytes 49160 | tf_op jit(solution)/shard_map/ppermute | solution.py:190
  40.1 9.2 %collective-permute-start.22 = (f32[32,128]{1,0:T(8,128)S(1)}, f32[32,128]{1,0:T(8,128)S(1)}, u32[]{:S(2)}, u32[]{:S(2)}) collective-permute-start(f32[32,128]{1,0:T(8,128)S(1)} %get-tuple-element.24), channel_id=1, source_target_pairs={{2,28},{5,27},{6,24},{7,25},{10,20},{13,19},{14,16},{15,17},{18,12... | collective-permute-start | bytes 49160 | tf_op jit(solution)/shard_map/ppermute | solution.py:190
  41.4 9.2 %collective-permute-start.21 = (f32[32,128]{1,0:T(8,128)S(1)}, f32[32,128]{1,0:T(8,128)S(1)}, u32[]{:S(2)}, u32[]{:S(2)}) collective-permute-start(f32[32,128]{1,0:T(8,128)S(1)} %get-tuple-element.25), channel_id=1, source_target_pairs={{2,24},{5,25},{6,28},{7,27},{10,16},{13,17},{14,20},{15,19},{18,8}... | collective-permute-start | bytes 49160 | tf_op jit(solution)/shard_map/ppermute | solution.py:190
  42.7 9.2 %collective-permute-start.20 = (f32[32,128]{1,0:T(8,128)S(1)}, f32[32,128]{1,0:T(8,128)S(1)}, u32[]{:S(2)}, u32[]{:S(2)}) collective-permute-start(f32[32,128]{1,0:T(8,128)S(1)} %get-tuple-element.26), channel_id=1, source_target_pairs={{2,20},{5,19},{6,16},{7,17},{10,28},{13,27},{14,24},{15,25},{18,4}... | collective-permute-start | bytes 49160 | tf_op jit(solution)/shard_map/ppermute | solution.py:190
  44.1 8.4 %collective-permute-start.19 = (f32[32,128]{1,0:T(8,128)S(1)}, f32[32,128]{1,0:T(8,128)S(1)}, u32[]{:S(2)}, u32[]{:S(2)}) collective-permute-start(f32[32,128]{1,0:T(8,128)S(1)} %get-tuple-element.27), channel_id=1, source_target_pairs={{2,16},{5,17},{6,20},{7,19},{10,24},{13,25},{14,28},{15,27},{18,0}... | collective-permute-start | bytes 49160 | tf_op jit(solution)/shard_map/ppermute | solution.py:190
  45.4 8.6 %collective-permute-start.18 = (f32[32,128]{1,0:T(8,128)S(1)}, f32[32,128]{1,0:T(8,128)S(1)}, u32[]{:S(2)}, u32[]{:S(2)}) collective-permute-start(f32[32,128]{1,0:T(8,128)S(1)} %get-tuple-element.28), channel_id=1, source_target_pairs={{2,12},{5,11},{6,8},{7,9},{10,4},{13,3},{14,0},{15,1},{18,28},{21,... | collective-permute-start | bytes 49160 | tf_op jit(solution)/shard_map/ppermute | solution.py:190
  49.4 6.5 %collective-permute-start.17 = (f32[32,128]{1,0:T(8,128)S(1)}, f32[32,128]{1,0:T(8,128)S(1)}, u32[]{:S(2)}, u32[]{:S(2)}) collective-permute-start(f32[32,128]{1,0:T(8,128)S(1)} %get-tuple-element.29), channel_id=1, source_target_pairs={{2,8},{5,9},{6,12},{7,11},{10,0},{13,1},{14,4},{15,3},{18,24},{21,... | collective-permute-start | bytes 49160 | tf_op jit(solution)/shard_map/ppermute | solution.py:190
  50.7 6.5 %collective-permute-start.16 = (f32[32,128]{1,0:T(8,128)S(1)}, f32[32,128]{1,0:T(8,128)S(1)}, u32[]{:S(2)}, u32[]{:S(2)}) collective-permute-start(f32[32,128]{1,0:T(8,128)S(1)} %get-tuple-element.30), channel_id=1, source_target_pairs={{2,4},{5,3},{6,0},{7,1},{10,12},{13,11},{14,8},{15,9},{18,20},{21,... | collective-permute-start | bytes 49160 | tf_op jit(solution)/shard_map/ppermute | solution.py:190

commit v2 on v0

--- a/solution.py
+++ b/solution.py
@@ -121,12 +121,9 @@
         return carry
 
     lax.fori_loop(0, (codes[2, 0] + GROUP - 1) // GROUP, one_group, 0)
-    me = lax.axis_index("pair")
-
     def give(chunk, carry):
-        device = lax.bitwise_xor(me, lax.rem(chunk, far) * NEAR + chunk // far)
         for tile in range(out_tiles):
-            result[device, tile * rows : (tile + 1) * rows, :] = totals[tile, pl.ds(chunk * rows, rows), :]
+            result[chunk, tile * rows : (tile + 1) * rows, :] = totals[tile, pl.ds(chunk * rows, rows), :]
         return carry
 
     lax.fori_loop(0, chunk_count, give, 0, unroll=min(chunk_count, 16))
@@ -150,12 +147,14 @@
     )(codes, blocks, halves)
 
 
-def from_partners(value, pairs, virts, masks):
-    received = []
-    for mask in masks:
-        routes = [(a * virts + b, (a ^ mask) * virts + (b ^ 1)) for a in range(pairs) for b in range(virts)]
-        received.append(lax.ppermute(value, ("pair", "virt"), routes))
-    return received
+def swap(value, pairs, virts, mask):
+    routes = [(a * virts + b, (a ^ mask) * virts + (b ^ 1)) for a in range(pairs) for b in range(virts)]
+    return lax.ppermute(value, ("pair", "virt"), routes)
+
+
+def swap_sum(parts, pairs, virts, masks):
+    received = [swap(part, pairs, virts, mask) for part, mask in zip(parts, masks)]
+    return sum(received[1:], received[0])
 
 
 def shards(t2_amplitudes, integral_tiles, out_tiles, in_tiles, tile_counts):
@@ -172,12 +171,13 @@
         mine,
         local_tiles,
     )
-    line = jnp.stack([own] + from_partners(mine, pairs, virts, range(NEAR, pairs, NEAR)))
-    gathered = jnp.concatenate([line] + from_partners(line, pairs, virts, range(1, NEAR)))
+    far_masks, near_masks = range(0, pairs, NEAR), range(NEAR)
+    line = jnp.stack([own] + [swap(mine, pairs, virts, mask) for mask in far_masks[1:]])
+    gathered = jnp.concatenate([line] + [swap(line, pairs, virts, mask) for mask in near_masks[1:]])
     blocks = lax.all_gather(gathered, "virt", axis=0)
     partial_sums = local_terms(codes, blocks, halves, rows, local_tiles)
-    received = lax.all_to_all(partial_sums, "pair", 0, 0)
-    summed = jnp.sum(received, axis=0)
+    line_sums = swap_sum(partial_sums.reshape((NEAR, pairs // NEAR) + mine.shape), pairs, virts, near_masks)
+    summed = swap_sum(line_sums, pairs, virts, far_masks)
     return summed.reshape(local_tiles, rows, W).transpose(1, 0, 2).reshape(rows, columns)
 
 

time: 35.1 us -> 36.1 us (1.028)
  blocking collectives: 17.5 us -> 2.18 us
  starting transfers between devices: 8.77 us -> 16.3 us
  waiting for transfers between devices: 5.11 us -> 12.2 us
  Pallas kernels: 2.34 us -> 3.72 us
    all_to_all x1 -> x0, blocking collectives: 15.3 us -> none  [shards(): received = lax.all_to_all(partial_sums, 'pair', 0, 0)]
    ppermute x6 -> x14, starting transfers between devices: 8.77 us -> 16.3 us  [swap(): return lax.ppermute(value, ('pair', 'virt'), routes)]
    ppermute x6 -> x14, waiting for transfers between devices: 5.11 us -> 12.2 us  [swap(): return lax.ppermute(value, ('pair', 'virt'), routes)]
    pallas_call x1, Pallas kernels: 1.1 us -> 2 us  [local_terms(): pl.pallas_call(ladder_kernel, out_shape=jax.ShapeDtypeStruct((chunk_count...]
    add x0 -> x2, other arithmetic: none -> 0.63 us  [swap_sum(): return sum(received[1:], received[0])]
    reduce_sum x1 -> x0, other arithmetic: 0.63 us -> none  [shards(): summed = jnp.sum(received, axis=0)]
    pallas_call x1, Pallas kernels: 1.24 us -> 1.71 us  [prepare(): pl.pallas_call(kernel, out_shape=(jax.ShapeDtypeStruct((slots, W, 2 * W),...]
  transfers between devices with their start and end apart: 6 -> 14, of which waited for: 3 -> 8; matrix products, arithmetic and copies ran while one was open for 0% -> 0% of each run, Pallas kernels for 4% -> 5%
where the time goes in v2:
time: 36.1 us; the launch traced here: 35.8 us
  starting transfers between devices  16.3 us (45%)
  waiting for transfers between devices  12.2 us (34%)
  Pallas kernels  3.72 us (10%)
  blocking collectives  2.18 us (6%)
  between operations  0.73 us (2%)
  other arithmetic  0.64 us (2%)
    ppermute x14, starting transfers between devices, swap(): return lax.ppermute(value, ('pair', 'virt'), routes)  16.3 us
    ppermute x14, waiting for transfers between devices, swap(): return lax.ppermute(value, ('pair', 'virt'), routes)  12.2 us
    all_gather x1, blocking collectives, shards(): blocks = lax.all_gather(gathered, 'virt', axis=0)  2.18 us
    pallas_call x1, Pallas kernels, local_terms(): pl.pallas_call(ladder_kernel, out_shape=jax.ShapeDtypeStruct((chunk_count...  2 us
    pallas_call x1, Pallas kernels, prepare(): pl.pallas_call(kernel, out_shape=(jax.ShapeDtypeStruct((slots, W, 2 * W),...  1.71 us
  transfers between devices with their start and end apart: 14, of which 8 were waited for; matrix products, arithmetic and copies ran while one was open for 0% of the time, Pallas kernels for 5%

profile of v2, /device:TPU:0, one launch (start us, length us, event | category | flops | bytes accessed | tf_op | source)
XLA Modules:
  0.0 35.8 jit_solution(11755409355310704456)
XLA Ops:
  0.0 4.5 %collective-permute-start.2 = (f32[32,128]{1,0:T(8,128)}, f32[32,128]{1,0:T(8,128)S(1)}, u32[]{:S(2)}, u32[]{:S(2)}) collective-permute-start(f32[32,128]{1,0:T(8,128)} %bitcast.36), channel_id=1, source_target_pairs={{0,25},{1,24},{2,27},{3,26},{4,29},{5,28},{6,31},{7,30},{8,17},{9,... | collective-permute-start | bytes 49160 | tf_op jit(solution)/shard_map/ppermute | solution.py:152
  4.5 0.0 collective-permute-start.1
  4.5 0.8 %collective-permute-start = (f32[32,128]{1,0:T(8,128)}, f32[32,128]{1,0:T(8,128)S(1)}, u32[]{:S(2)}, u32[]{:S(2)}) collective-permute-start(f32[32,128]{1,0:T(8,128)} %bitcast.38), channel_id=1, source_target_pairs={{0,9},{1,8},{2,11},{3,10},{4,13},{5,12},{6,15},{7,14},{8,1},{9,0},... | collective-permute-start | bytes 49160 | tf_op jit(solution)/shard_map/ppermute | solution.py:152
  6.0 1.7 %shard_map.55 = (bf16[32,128,256]{2,1,0:T(8,128)(2,1)S(1)}, s32[3,32]{1,0:T(4,128)S(1)}, f32[32,128]{1,0:T(8,128)S(1)}) custom-call(s32[1,1]{1,0:T(1,128)S(6)} %copy.16.refs_0_, s32[1,32]{1,0:T(1,128)} %bitcast.40, s32[1,32]{1,0:T(1,128)} %bitcast.41, f32[32,128,128]{2,1,0:T(8,128)} %bitcast.32, f32[32,128]{1,0:T(8,128)} %bitcast.39), custom_call_target="tpu_custom_call" | custom-call | flops 2097152 | bytes 4194304 | tf_op jit(solution)/shard_map/pallas_call | solution.py:64
  7.7 0.0 collective-permute-done.2
  7.7 1.2 %collective-permute-done.1 = f32[32,128]{1,0:T(8,128)S(1)} collective-permute-done((f32[32,128]{1,0:T(8,128)}, f32[32,128]{1,0:T(8,128)S(1)}, u32[]{:S(2)}, u32[]{:S(2)}) %collective-permute-start.1) | collective-permute-done | bytes 16416 | tf_op jit(solution)/shard_map/ppermute | solution.py:152
  8.9 0.0 collective-permute-done
  8.9 2.7 %collective-permute-start.5 = (f32[4,32,128]{2,1,0:T(8,128)S(1)}, f32[4,32,128]{2,1,0:T(8,128)S(1)}, u32[]{:S(2)}, u32[]{:S(2)}) collective-permute-start(f32[4,32,128]{2,1,0:T(8,128)S(1)} %pad_maximum_fusion), channel_id=1, source_target_pairs={{0,7},{1,6},{2,5},{3,4},{4,3},{5,2},{6,1},{7,0},{8,15},{9,14},{10,... | collective-permute-start | bytes 196616 | tf_op jit(solution)/shard_map/ppermute | solution.py:152
  11.6 0.1 collective-permute-start.4
  11.6 0.7 %collective-permute-start.3 = (f32[4,32,128]{2,1,0:T(8,128)S(1)}, f32[4,32,128]{2,1,0:T(8,128)S(1)}, u32[]{:S(2)}, u32[]{:S(2)}) collective-permute-start(f32[4,32,128]{2,1,0:T(8,128)S(1)} %pad_maximum_fusion), channel_id=1, source_target_pairs={{0,3},{1,2},{2,1},{3,0},{4,7},{5,6},{6,5},{7,4},{8,11},{9,10},{10,... | collective-permute-start | bytes 196616 | tf_op jit(solution)/shard_map/ppermute | solution.py:152
  12.3 3.0 %collective-permute-done.3 = f32[4,32,128]{2,1,0:T(8,128)S(1)} collective-permute-done((f32[4,32,128]{2,1,0:T(8,128)S(1)}, f32[4,32,128]{2,1,0:T(8,128)S(1)}, u32[]{:S(2)}, u32[]{:S(2)}) %collective-permute-start.3) | collective-permute-done | bytes 65568 | tf_op jit(solution)/shard_map/ppermute | solution.py:152
  15.3 0.5 %collective-permute-done.4 = f32[4,32,128]{2,1,0:T(8,128)S(1)} collective-permute-done((f32[4,32,128]{2,1,0:T(8,128)S(1)}, f32[4,32,128]{2,1,0:T(8,128)S(1)}, u32[]{:S(2)}, u32[]{:S(2)}) %collective-permute-start.4) | collective-permute-done | bytes 65568 | tf_op jit(solution)/shard_map/ppermute | solution.py:152
  15.8 0.0 collective-permute-done.5
  15.8 2.2 %all-gather = f32[32,32,128]{2,1,0:T(8,128)S(1)} all-gather(f32[16,32,128]{2,1,0:T(8,128)S(1)} %constant_dynamic-update-slice_fusion), channel_id=2, replica_groups=mesh['pair'=16,'virt'=2] {'virt'}, dimensions={0}, use_global_device_ids=true | all-gather | bytes 786432 | tf_op jit(solution)/shard_map/all_gather | solution.py:177
  18.0 2.0 %shard_map.56 = f32[16,32,128]{2,1,0:T(8,128)S(1)} custom-call(s32[3,32]{1,0:T(4,128)S(1)} %get-tuple-element.8.codes, f32[2,16,32,128]{3,2,1,0:T(8,128)S(1)} %bitcast.30, bf16[32,128,256]{2,1,0:T(8,128)(2,1)S(1)} %get-tuple-element.10.halves), custom_call_target="tpu_custom_call" | custom-call | tf_op jit(solution)/shard_map/pallas_call | solution.py:136
  20.1 0.2 collective-permute-start.7
  20.3 1.3 %collective-permute-start.9 = (f32[4,32,128]{2,1,0:T(8,128)S(1)}, f32[4,32,128]{2,1,0:T(8,128)S(1)}, u32[]{:S(2)}, u32[]{:S(2)}) collective-permute-start(f32[4,32,128]{2,1,0:T(8,128)S(1)} %get-tuple-element.12), channel_id=1, source_target_pairs={{0,7},{1,6},{2,5},{3,4},{4,3},{5,2},{6,1},{7,0},{8,15},{9,14},{10,... | collective-permute-start | bytes 196616 | tf_op jit(solution)/shard_map/ppermute | solution.py:152
  21.6 0.5 %collective-permute-start.8 = (f32[4,32,128]{2,1,0:T(8,128)S(1)}, f32[4,32,128]{2,1,0:T(8,128)S(1)}, u32[]{:S(2)}, u32[]{:S(2)}) collective-permute-start(f32[4,32,128]{2,1,0:T(8,128)S(1)} %get-tuple-element.13), channel_id=1, source_target_pairs={{0,5},{1,4},{2,7},{3,6},{4,1},{5,0},{6,3},{7,2},{8,13},{9,12},{10,... | collective-permute-start | bytes 196616 | tf_op jit(solution)/shard_map/ppermute | solution.py:152
  22.2 1.3 %collective-permute-start.6 = (f32[4,32,128]{2,1,0:T(8,128)S(1)}, f32[4,32,128]{2,1,0:T(8,128)S(1)}, u32[]{:S(2)}, u32[]{:S(2)}) collective-permute-start(f32[4,32,128]{2,1,0:T(8,128)S(1)} %get-tuple-element.14), channel_id=1, source_target_pairs={{0,1},{1,0},{2,3},{3,2},{4,5},{5,4},{6,7},{7,6},{8,9},{9,8},{10,11... | collective-permute-start | bytes 196616 | tf_op jit(solution)/shard_map/ppermute | solution.py:152
  23.5 0.5 %collective-permute-done.7 = f32[4,32,128]{2,1,0:T(8,128)S(1)} collective-permute-done((f32[4,32,128]{2,1,0:T(8,128)S(1)}, f32[4,32,128]{2,1,0:T(8,128)S(1)}, u32[]{:S(2)}, u32[]{:S(2)}) %collective-permute-start.7) | collective-permute-done | bytes 65568 | tf_op jit(solution)/shard_map/ppermute | solution.py:152
  23.9 1.4 %collective-permute-done.9 = f32[4,32,128]{2,1,0:T(8,128)S(1)} collective-permute-done((f32[4,32,128]{2,1,0:T(8,128)S(1)}, f32[4,32,128]{2,1,0:T(8,128)S(1)}, u32[]{:S(2)}, u32[]{:S(2)}) %collective-permute-start.9) | collective-permute-done | bytes 65568 | tf_op jit(solution)/shard_map/ppermute | solution.py:152
  25.4 1.7 %collective-permute-done.8 = f32[4,32,128]{2,1,0:T(8,128)S(1)} collective-permute-done((f32[4,32,128]{2,1,0:T(8,128)S(1)}, f32[4,32,128]{2,1,0:T(8,128)S(1)}, u32[]{:S(2)}, u32[]{:S(2)}) %collective-permute-start.8) | collective-permute-done | bytes 65568 | tf_op jit(solution)/shard_map/ppermute | solution.py:152
  27.0 0.0 collective-permute-done.6
  27.1 0.3 collective-permute-start.11
  27.4 3.8 %collective-permute-start.13 = (f32[32,128]{1,0:T(8,128)S(1)}, f32[32,128]{1,0:T(8,128)S(1)}, u32[]{:S(2)}, u32[]{:S(2)}) collective-permute-start(f32[32,128]{1,0:T(8,128)S(1)} %get-tuple-element.16), channel_id=1, source_target_pairs={{0,25},{1,24},{2,27},{3,26},{4,29},{5,28},{6,31},{7,30},{8,17},{9,... | collective-permute-start | bytes 49160 | tf_op jit(solution)/shard_map/ppermute | solution.py:152
  31.2 0.0 collective-permute-start.12
  31.2 0.1 collective-permute-start.10
  31.2 0.0 collective-permute-done.11
  31.2 1.5 %collective-permute-done.13 = f32[32,128]{1,0:T(8,128)S(1)} collective-permute-done((f32[32,128]{1,0:T(8,128)S(1)}, f32[32,128]{1,0:T(8,128)S(1)}, u32[]{:S(2)}, u32[]{:S(2)}) %collective-permute-start.13) | collective-permute-done | bytes 16416 | tf_op jit(solution)/shard_map/ppermute | solution.py:152
  32.8 2.4 %collective-permute-done.12 = f32[32,128]{1,0:T(8,128)S(1)} collective-permute-done((f32[32,128]{1,0:T(8,128)S(1)}, f32[32,128]{1,0:T(8,128)S(1)}, u32[]{:S(2)}, u32[]{:S(2)}) %collective-permute-start.12) | collective-permute-done | bytes 16416 | tf_op jit(solution)/shard_map/ppermute | solution.py:152
  35.2 0.0 collective-permute-done.10
  35.2 0.6 %add_add_fusion.1 = f32[32,128]{1,0:T(8,128)} fusion(f32[32,128]{1,0:T(8,128)S(1)} %collective-permute-done.13, f32[32,128]{1,0:T(8,128)S(1)} %collective-permute-done.12, f32[32,128]{1,0:T(8,128)S(1)} %collective-permute-done.10, f32[32,128]{1,0:T(8,128)S(1)} %collective-permute-done.11), kind=kLoop, calls=%fused_computation.13 | loop fusion | flops 12288 | bytes 81920 | tf_op jit(solution)/shard_map/add | solution.py:157
  (11 shorter events, 0.1 us)
Async XLA Ops:
  0.0 7.7 %collective-permute-start.2 = (f32[32,128]{1,0:T(8,128)}, f32[32,128]{1,0:T(8,128)S(1)}, u32[]{:S(2)}, u32[]{:S(2)}) collective-permute-start(f32[32,128]{1,0:T(8,128)} %bitcast.36), channel_id=1, source_target_pairs={{0,25},{1,24},{2,27},{3,26},{4,29},{5,28},{6,31},{7,30},{8,17},{9,... | collective-permute-start | bytes 49160 | tf_op jit(solution)/shard_map/ppermute | solution.py:152
  4.5 4.4 %collective-permute-start.1 = (f32[32,128]{1,0:T(8,128)}, f32[32,128]{1,0:T(8,128)S(1)}, u32[]{:S(2)}, u32[]{:S(2)}) collective-permute-start(f32[32,128]{1,0:T(8,128)} %bitcast.37), channel_id=1, source_target_pairs={{0,17},{1,16},{2,19},{3,18},{4,21},{5,20},{6,23},{7,22},{8,25},{9,... | collective-permute-start | bytes 49160 | tf_op jit(solution)/shard_map/ppermute | solution.py:152
  4.5 4.4 %collective-permute-start = (f32[32,128]{1,0:T(8,128)}, f32[32,128]{1,0:T(8,128)S(1)}, u32[]{:S(2)}, u32[]{:S(2)}) collective-permute-start(f32[32,128]{1,0:T(8,128)} %bitcast.38), channel_id=1, source_target_pairs={{0,9},{1,8},{2,11},{3,10},{4,13},{5,12},{6,15},{7,14},{8,1},{9,0},... | collective-permute-start | bytes 49160 | tf_op jit(solution)/shard_map/ppermute | solution.py:152
  8.9 6.9 %collective-permute-start.5 = (f32[4,32,128]{2,1,0:T(8,128)S(1)}, f32[4,32,128]{2,1,0:T(8,128)S(1)}, u32[]{:S(2)}, u32[]{:S(2)}) collective-permute-start(f32[4,32,128]{2,1,0:T(8,128)S(1)} %pad_maximum_fusion), channel_id=1, source_target_pairs={{0,7},{1,6},{2,5},{3,4},{4,3},{5,2},{6,1},{7,0},{8,15},{9,14},{10,... | collective-permute-start | bytes 196616 | tf_op jit(solution)/shard_map/ppermute | solution.py:152
  11.6 4.3 %collective-permute-start.4 = (f32[4,32,128]{2,1,0:T(8,128)S(1)}, f32[4,32,128]{2,1,0:T(8,128)S(1)}, u32[]{:S(2)}, u32[]{:S(2)}) collective-permute-start(f32[4,32,128]{2,1,0:T(8,128)S(1)} %pad_maximum_fusion), channel_id=1, source_target_pairs={{0,5},{1,4},{2,7},{3,6},{4,1},{5,0},{6,3},{7,2},{8,13},{9,12},{10,... | collective-permute-start | bytes 196616 | tf_op jit(solution)/shard_map/ppermute | solution.py:152
  11.6 3.7 %collective-permute-start.3 = (f32[4,32,128]{2,1,0:T(8,128)S(1)}, f32[4,32,128]{2,1,0:T(8,128)S(1)}, u32[]{:S(2)}, u32[]{:S(2)}) collective-permute-start(f32[4,32,128]{2,1,0:T(8,128)S(1)} %pad_maximum_fusion), channel_id=1, source_target_pairs={{0,3},{1,2},{2,1},{3,0},{4,7},{5,6},{6,5},{7,4},{8,11},{9,10},{10,... | collective-permute-start | bytes 196616 | tf_op jit(solution)/shard_map/ppermute | solution.py:152
  20.1 3.9 %collective-permute-start.7 = (f32[4,32,128]{2,1,0:T(8,128)S(1)}, f32[4,32,128]{2,1,0:T(8,128)S(1)}, u32[]{:S(2)}, u32[]{:S(2)}) collective-permute-start(f32[4,32,128]{2,1,0:T(8,128)S(1)} %get-tuple-element.11), channel_id=1, source_target_pairs={{0,3},{1,2},{2,1},{3,0},{4,7},{5,6},{6,5},{7,4},{8,11},{9,10},{10,... | collective-permute-start | bytes 196616 | tf_op jit(solution)/shard_map/ppermute | solution.py:152
  20.3 5.0 %collective-permute-start.9 = (f32[4,32,128]{2,1,0:T(8,128)S(1)}, f32[4,32,128]{2,1,0:T(8,128)S(1)}, u32[]{:S(2)}, u32[]{:S(2)}) collective-permute-start(f32[4,32,128]{2,1,0:T(8,128)S(1)} %get-tuple-element.12), channel_id=1, source_target_pairs={{0,7},{1,6},{2,5},{3,4},{4,3},{5,2},{6,1},{7,0},{8,15},{9,14},{10,... | collective-permute-start | bytes 196616 | tf_op jit(solution)/shard_map/ppermute | solution.py:152
  21.6 5.4 %collective-permute-start.8 = (f32[4,32,128]{2,1,0:T(8,128)S(1)}, f32[4,32,128]{2,1,0:T(8,128)S(1)}, u32[]{:S(2)}, u32[]{:S(2)}) collective-permute-start(f32[4,32,128]{2,1,0:T(8,128)S(1)} %get-tuple-element.13), channel_id=1, source_target_pairs={{0,5},{1,4},{2,7},{3,6},{4,1},{5,0},{6,3},{7,2},{8,13},{9,12},{10,... | collective-permute-start | bytes 196616 | tf_op jit(solution)/shard_map/ppermute | solution.py:152
  22.2 4.9 %collective-permute-start.6 = (f32[4,32,128]{2,1,0:T(8,128)S(1)}, f32[4,32,128]{2,1,0:T(8,128)S(1)}, u32[]{:S(2)}, u32[]{:S(2)}) collective-permute-start(f32[4,32,128]{2,1,0:T(8,128)S(1)} %get-tuple-element.14), channel_id=1, source_target_pairs={{0,1},{1,0},{2,3},{3,2},{4,5},{5,4},{6,7},{7,6},{8,9},{9,8},{10,11... | collective-permute-start | bytes 196616 | tf_op jit(solution)/shard_map/ppermute | solution.py:152
  27.1 4.2 %collective-permute-start.11 = (f32[32,128]{1,0:T(8,128)S(1)}, f32[32,128]{1,0:T(8,128)S(1)}, u32[]{:S(2)}, u32[]{:S(2)}) collective-permute-start(f32[32,128]{1,0:T(8,128)S(1)} %get-tuple-element.15), channel_id=1, source_target_pairs={{0,9},{1,8},{2,11},{3,10},{4,13},{5,12},{6,15},{7,14},{8,1},{9,0},... | collective-permute-start | bytes 49160 | tf_op jit(solution)/shard_map/ppermute | solution.py:152
  27.4 5.4 %collective-permute-start.13 = (f32[32,128]{1,0:T(8,128)S(1)}, f32[32,128]{1,0:T(8,128)S(1)}, u32[]{:S(2)}, u32[]{:S(2)}) collective-permute-start(f32[32,128]{1,0:T(8,128)S(1)} %get-tuple-element.16), channel_id=1, source_target_pairs={{0,25},{1,24},{2,27},{3,26},{4,29},{5,28},{6,31},{7,30},{8,17},{9,... | collective-permute-start | bytes 49160 | tf_op jit(solution)/shard_map/ppermute | solution.py:152
  31.2 4.1 %collective-permute-start.12 = (f32[32,128]{1,0:T(8,128)S(1)}, f32[32,128]{1,0:T(8,128)S(1)}, u32[]{:S(2)}, u32[]{:S(2)}) collective-permute-start(f32[32,128]{1,0:T(8,128)S(1)} %get-tuple-element.17), channel_id=1, source_target_pairs={{0,17},{1,16},{2,19},{3,18},{4,21},{5,20},{6,23},{7,22},{8,25},{9,... | collective-permute-start | bytes 49160 | tf_op jit(solution)/shard_map/ppermute | solution.py:152
  31.2 4.1 %collective-permute-start.10 = (f32[32,128]{1,0:T(8,128)S(1)}, f32[32,128]{1,0:T(8,128)S(1)}, u32[]{:S(2)}, u32[]{:S(2)}) collective-permute-start(f32[32,128]{1,0:T(8,128)S(1)} %get-tuple-element.18), channel_id=1, source_target_pairs={{0,1},{1,0},{2,3},{3,2},{4,5},{5,4},{6,7},{7,6},{8,9},{9,8},{10,11... | collective-permute-start | bytes 49160 | tf_op jit(solution)/shard_map/ppermute | solution.py:152
